TPU v7x, 32 devices: a whole 2x2x4 slice. The times are simulated.
32 devices in a mesh: rep: 2 (over x), gx: 8 (over z, y), yz: 2 (over core).
Axes of the slice: x: 2, y: 2, z: 4, core: 2. Of those that a mesh axis runs over, the one named last changes fastest.
Arguments:
- hidden: bfloat16 [2, 32, 16384], P(None, 'rep', 'gx'), parts along dimension 1, may hold values from -80 to 80
- norm_gain: float32 [16384], P('gx'), may hold values from 0.5 to 1.5
- query_weight: bfloat16 [16384, 8192], P('gx', 'yz'), may hold values from -0.046875 to 0.046875
- key_matrix: bfloat16 [16384, 512], P('gx', 'yz'), may hold values from -0.046875 to 0.046875
- value_matrix: bfloat16 [16384, 512], P('gx', 'yz'), may hold values from -0.046875 to 0.046875
- output_weight: bfloat16 [8192, 16384], P('yz', 'gx'), may hold values from -0.0625 to 0.0625
- key_cache_rows: bfloat16 [32, 2048, 512], P(('rep', 'gx', 'yz')), parts along dimension 0, may hold values from -2500 to 2500
- value_cache_rows: bfloat16 [32, 2048, 512], P(('rep', 'gx', 'yz')), parts along dimension 0, may hold values from -6 to 6
- lengths: int32 [32], P(('rep', 'gx', 'yz')), parts along dimension 0, may hold values from 2 to 2046, as said below
- positions: int32 [32], P('rep'), parts along dimension 0, may hold values from 0 to 1023
Outputs:
- out: bfloat16 [2, 32, 16384], P(None, 'rep', 'gx'), parts along dimension 1
- new_keys: bfloat16 [2, 32, 512], P(None, ('rep', 'gx', 'yz')), parts along dimension 1
- new_values: bfloat16 [2, 32, 512], P(None, ('rep', 'gx', 'yz')), parts along dimension 1
There are 2 independent parts, one for each index of `rep`. A program takes and returns all parts, laid end to end along the dimension named above; an argument that names none is the same for every part. Nothing has to cross between parts.
Inputs may be any that keep to these rules, and one draw needn't show every extreme that they name: Row r has lengths[r] valid cached entries at cache slots 0 to lengths[r] - 1; some row holds 2046.
All inputs are finite; a program needn't handle non-finite values.
Results may differ from a plain program's by a relative error of at most 0.0051.
Values may be sent and summed in bfloat16 or wider, within the bound.
A program may use at most 128 MiB of HBM per device.

v0:
```python
import jax
import jax.numpy as jnp
from jax import lax
from jax.sharding import PartitionSpec as P

MODEL_WIDTH = 16384
QUERY_HEADS = 64
KEY_VALUE_HEADS = 4
HEAD_SIZE = 128
STEPS = 2
CONTEXT_SLOTS = 2048


def rotate(values, offsets):
    half = HEAD_SIZE // 2
    filled_count = values.shape[0]
    heads = values.shape[1] // HEAD_SIZE
    freq = 500000.0 ** (-2.0 * jnp.arange(half, dtype=jnp.float32) / HEAD_SIZE)
    angles = offsets.astype(jnp.float32)[:, None] * freq[None, :]
    cosine = jnp.cos(angles)[:, None, :]
    sine = jnp.sin(angles)[:, None, :]
    split = values.reshape(filled_count, heads, HEAD_SIZE)
    first = split[:, :, :half]
    second = split[:, :, half:]
    joined = jnp.concatenate(
        [first * cosine - second * sine, second * cosine + first * sine], axis=2
    )
    return joined.reshape(filled_count, heads * HEAD_SIZE)


def attend(queries, row_keys, row_values, newest_keys, newest_values, length):
    group_size = QUERY_HEADS // KEY_VALUE_HEADS
    scale = HEAD_SIZE ** (-0.5)
    grouped = queries.reshape(STEPS, KEY_VALUE_HEADS, group_size, HEAD_SIZE)
    grouped = grouped.transpose(1, 0, 2, 3).reshape(
        KEY_VALUE_HEADS, STEPS * group_size, HEAD_SIZE
    )
    valid = jnp.arange(CONTEXT_SLOTS) < length
    query_step = jnp.arange(STEPS * group_size) // group_size
    seen = jnp.arange(STEPS)[None, :] <= query_step[:, None]
    results = []
    for head in range(KEY_VALUE_HEADS):
        part = slice(head * HEAD_SIZE, (head + 1) * HEAD_SIZE)
        own = grouped[head]
        cached = scale * lax.dot_general(
            own, row_keys[:, part], (((1,), (1,)), ((), ())), preferred_element_type=jnp.float32
        )
        recent = scale * lax.dot_general(
            own, newest_keys[:, part], (((1,), (1,)), ((), ())), preferred_element_type=jnp.float32
        )
        cached = jnp.where(valid[None, :], cached, -jnp.inf)
        recent = jnp.where(seen, recent, -jnp.inf)
        highest = jnp.maximum(
            jnp.max(cached, axis=1, keepdims=True), jnp.max(recent, axis=1, keepdims=True)
        )
        cached_w = jnp.exp(cached - highest)
        recent_w = jnp.exp(recent - highest)
        total = jnp.sum(cached_w, axis=1) + jnp.sum(recent_w, axis=1)
        weighted = jnp.dot(
            cached_w.astype(jnp.bfloat16), row_values[:, part], preferred_element_type=jnp.float32
        ) + jnp.dot(
            recent_w.astype(jnp.bfloat16),
            newest_values[:, part],
            preferred_element_type=jnp.float32,
        )
        results.append((weighted / total[:, None]).astype(jnp.bfloat16))
    joined = jnp.stack(results).reshape(KEY_VALUE_HEADS, STEPS, group_size, HEAD_SIZE)
    return joined.transpose(1, 0, 2, 3).reshape(STEPS, QUERY_HEADS * HEAD_SIZE)


def per_device(
    hidden,
    norm_gain,
    query_weight,
    key_matrix,
    value_matrix,
    output_weight,
    key_cache_rows,
    value_cache_rows,
    lengths,
    positions,
):
    batch_rows = hidden.shape[1]
    width = hidden.shape[2]
    share = batch_rows // lax.axis_size("gx")
    first_row = lax.axis_index("gx") * share
    query_cols = query_weight.shape[1]
    key_cols = key_matrix.shape[1]
    own_positions = lax.dynamic_slice_in_dim(positions, first_row, share, 0)
    inputs = hidden.transpose(1, 0, 2).reshape(batch_rows * STEPS, width).astype(jnp.float32)
    squares = jnp.sum(inputs * inputs, axis=1, keepdims=True)
    scaled = (inputs * norm_gain[None, :]).astype(jnp.bfloat16)
    sums = jnp.concatenate(
        [
            jnp.dot(scaled, query_weight, preferred_element_type=jnp.float32),
            jnp.dot(scaled, key_matrix, preferred_element_type=jnp.float32),
            jnp.dot(scaled, value_matrix, preferred_element_type=jnp.float32),
            jnp.broadcast_to(squares, (batch_rows * STEPS, HEAD_SIZE)),
        ],
        axis=1,
    )
    own = lax.psum_scatter(sums, "gx", scatter_dimension=0, tiled=True)
    cols = query_cols + 2 * key_cols
    inverse = lax.rsqrt(own[:, cols : cols + 1] / MODEL_WIDTH + 1e-05)
    projected = own[:, :cols] * inverse
    offsets = (own_positions[:, None] + jnp.arange(STEPS)[None, :]).reshape(share * STEPS)
    turned = rotate(projected[:, : query_cols + key_cols], offsets).astype(jnp.bfloat16)
    new_value = projected[:, query_cols + key_cols :].astype(jnp.bfloat16)
    packed = jnp.concatenate([turned, new_value], axis=1)
    halves = lax.axis_size("yz")
    swapped = lax.all_to_all(
        packed.reshape(halves, STEPS, cols), "yz", split_axis=0, concat_axis=0, tiled=True
    )
    swapped = swapped.transpose(1, 0, 2)
    row_query = swapped[:, :, :query_cols].reshape(STEPS, halves * query_cols)
    row_key = swapped[:, :, query_cols : query_cols + key_cols].reshape(STEPS, halves * key_cols)
    row_value = swapped[:, :, query_cols + key_cols :].reshape(STEPS, halves * key_cols)
    attended = attend(
        row_query, key_cache_rows[0], value_cache_rows[0], row_key, row_value, lengths[0]
    )
    head_pair = lax.all_to_all(attended, "yz", split_axis=1, concat_axis=0, tiled=True)
    gathered = lax.all_gather(head_pair, "gx", axis=0, tiled=True)
    partial_out = jnp.dot(gathered, output_weight, preferred_element_type=jnp.float32)
    mixed = inputs + lax.psum(partial_out.astype(jnp.bfloat16), "yz").astype(jnp.float32)
    out = mixed.astype(jnp.bfloat16).reshape(batch_rows, STEPS, width).transpose(1, 0, 2)
    return (out, row_key[:, None, :], row_value[:, None, :])


def solution(mesh):
    in_specs = (
        P(None, "rep", "gx"),
        P("gx"),
        P("gx", "yz"),
        P("gx", "yz"),
        P("gx", "yz"),
        P("yz", "gx"),
        P(("rep", "gx", "yz"), None, None),
        P(("rep", "gx", "yz"), None, None),
        P(("rep", "gx", "yz")),
        P("rep"),
    )
    out_specs = (
        P(None, "rep", "gx"),
        P(None, ("rep", "gx", "yz"), None),
        P(None, ("rep", "gx", "yz"), None),
    )
    return jax.shard_map(
        per_device, mesh=mesh, in_specs=in_specs, out_specs=out_specs, check_vma=False
    )
```

profile of v0, /device:TPU:0, one launch (start us, length us, event | category | flops | bytes accessed | tf_op | source)
XLA Modules:
  0.0 180.8 jit_solution(5685003988207097043)
XLA Ops:
  7.2 0.0 copy-start
  7.2 0.0 all-reduce.6.cloned.1.call-start
  7.2 1.0 convert_bitcast_fusion
  8.2 1.0 fusion.28
  9.2 0.2 copy.30
  9.5 0.2 reshape.187
  9.6 0.7 multiply_convert_fusion
  10.4 0.0 copy-start.3
  10.4 8.8 %fusion.82 = f32[32,4096]{1,0:T(8,128)S(1)} fusion(bf16[32,2048]{1,0:T(8,128)(2,1)S(1)} %multiply_convert_fusion, bf16[2048,4096]{1,0:T(8,128)(2,1)} %param.12), kind=kOutput, calls=%fused_computation.120 | convolution fusion | flops 536870912 | bytes 17432576 | tf_op jit(solution)/shard_map/dot_general | solution.py:95
  19.2 0.0 copy-start.6
  19.2 0.0 copy-start.7
  19.3 0.3 fusion.83
  19.5 0.0 copy-done.3
  19.6 0.3 fusion.84
  19.8 0.1 copy.31
  19.9 0.1 broadcast_in_dim.36
  20.0 0.1 broadcast_in_dim.37
  20.1 0.9 pad_maximum_fusion
  21.0 0.0 all-reduce.6.cloned.1.call-update
  21.0 0.0 all-reduce.4.cloned.1.call-start
  21.1 0.1 dynamic_slice.3
  21.1 0.1 add_convert_fusion.2
  21.2 0.1 convert_element_type.82
  22.1 0.6 dynamic-slice
  23.4 0.1 multiply_cosine_fusion
  23.5 73.4 %all-reduce.6.cloned.1.call-done = f32[32,4736]{1,0:T(8,128)} async-done(((f32[32,4736]{1,0:T(8,128)}), f32[32,4736]{1,0:T(8,128)}) %all-reduce.6.cloned.1.call-update) | async-done | bytes 606224
  96.9 0.9 fusion.47
  97.8 1.0 dynamic-slice_multiply_fusion
  98.8 0.6 slice.121
  99.4 0.9 reshape.182
  100.3 0.1 subtract_convert_fusion
  100.4 0.1 maximum_bitcast_fusion
  100.6 3.8 %all_to_all.24 = bf16[2,2,4608]{2,1,0:T(2,128)(2,1)S(1)} all-to-all(bf16[2,2,4608]{2,1,0:T(2,128)(2,1)S(1)} %reshape.183), channel_id=1, replica_groups=mesh['rep'=2,'gx'=8,'yz'=2] {'yz'}, dimensions={0} | all-to-all | bytes 73728 | tf_op jit(solution)/shard_map/all_to_all | solution.py:111
  104.3 0.0 copy-start.4
  104.5 0.0 copy-start.2
  104.5 0.1 fusion.81
  104.6 0.1 fusion.79
  104.8 0.4 fusion.80
  105.2 0.4 fusion.78
  105.6 0.2 fusion.29
  105.8 1.3 fusion.25
  107.1 0.2 fusion.31
  107.3 0.3 fusion.22
  107.6 0.1 fusion.77
  107.8 0.4 fusion.76
  108.2 0.2 fusion.33
  108.4 0.3 fusion.19
  108.7 0.1 fusion.75
  108.8 0.4 fusion.74
  109.2 0.2 fusion.35
  109.4 0.3 fusion.16
  109.8 0.2 fusion.8
  110.0 0.2 fusion.9
  110.2 0.2 fusion.10
  110.5 0.2 fusion.11
  110.7 3.7 %all_to_all.25 = bf16[2,2,4096]{2,0,1:T(2,128)(2,1)S(1)} all-to-all(bf16[2,2,4096]{2,0,1:T(2,128)(2,1)S(1)} %copy.37), channel_id=1, replica_groups=mesh['rep'=2,'gx'=8,'yz'=2] {'yz'}, dimensions={1} | all-to-all | bytes 65536 | tf_op jit(solution)/shard_map/all_to_all | solution.py:121
  114.5 30.9 %all-gather = bf16[8,4,4096]{2,1,0:T(4,128)(2,1)S(1)} all-gather(bf16[1,4,4096]{2,1,0:T(4,128)(2,1)S(1)} %reshape.188), channel_id=1, replica_groups=mesh['rep'=2,'gx'=8,'yz'=2] {'gx'}, dimensions={0}, use_global_device_ids=true | all-gather | bytes 294912 | tf_op jit(solution)/shard_map/all_gather | solution.py:122
  145.4 0.1 reshape.189
  145.5 9.4 %convolution_convert_fusion = bf16[32,2048]{1,0:T(8,128)(2,1)} fusion(bf16[32,4096]{1,0:T(8,128)(2,1)S(1)} %reshape.189, bf16[4096,2048]{1,0:T(8,128)(2,1)} %param.15), kind=kOutput, calls=%fused_computation.8 | convolution fusion | flops 536936448 | bytes 17170432 | tf_op jit(solution)/shard_map/dot_general | solution.py:123
  154.9 0.0 all-reduce.4.cloned.1.call-update
  154.9 17.3 %all-reduce.4.cloned.1.call-done = bf16[32,2048]{1,0:T(8,128)(2,1)} async-done(((bf16[32,2048]{1,0:T(8,128)(2,1)}), bf16[32,2048]{1,0:T(8,128)(2,1)}) %all-reduce.4.cloned.1.call-update) | async-done | bytes 131088 | tf_op jit(solution)/shard_map/psum | solution.py:124
  172.2 0.9 add_convert_fusion
  173.1 0.1 reshape.186
  173.2 0.7 copy.42
  (37 shorter events, 0.5 us)
Async XLA Ops:
  7.2 12.1 %copy-start = (bf16[2048,256]{1,0:T(8,128)(2,1)S(1)}, bf16[2048,256]{1,0:T(8,128)(2,1)}, u32[]{:S(2)}) copy-start(bf16[2048,256]{1,0:T(8,128)(2,1)} %param.13) | copy-start | bytes 3145732
  7.2 89.7 %all-reduce.6.cloned.1.call-start = ((), (), s32[]{:S(2)}) async-start(), calls=%async_computation.3 | async-start | bytes 1212416
  10.4 9.2 %copy-start.3 = (bf16[2048,256]{1,0:T(8,128)(2,1)S(1)}, bf16[2048,256]{1,0:T(8,128)(2,1)}, u32[]{:S(2)}) copy-start(bf16[2048,256]{1,0:T(8,128)(2,1)} %param.14) | copy-start | bytes 3145732
  19.2 1.8 %copy-start.6 = (s32[16]{0:T(128)S(1)}, s32[16]{0:T(128)}, u32[]{:S(2)}) copy-start(s32[16]{0:T(128)} %param.19) | copy-start | bytes 196
  19.2 2.9 %copy-start.7 = (u32[32]{0:T(128)S(1)}, u32[32]{0:T(128)}, u32[]{:S(2)}) copy-start(u32[32]{0:T(128)} %constant.52) | copy-start | bytes 388
  21.0 83.8 %copy-start.1 = (bf16[1,2048,512]{2,1,0:T(8,128)(2,1)S(1)}, bf16[1,2048,512]{2,1,0:T(8,128)(2,1)}, u32[]{:S(2)}) copy-start(bf16[1,2048,512]{2,1,0:T(8,128)(2,1)} %param.16) | copy-start | bytes 6291460
  21.0 151.2 %all-reduce.4.cloned.1.call-start = ((), (), s32[]{:S(2)}) async-start(), calls=%async_computation.2 | async-start | bytes 262144 | tf_op jit(solution)/shard_map/psum | solution.py:124
  104.3 4.3 %copy-start.5 = (bf16[2,2,256]{2,0,1:T(2,128)(2,1)}, bf16[2,2,256]{2,0,1:T(2,128)(2,1)S(1)}, u32[]{:S(2)}) copy-start(bf16[2,2,256]{2,0,1:T(2,128)(2,1)S(1)} %get-tuple-element.6) | copy-start | bytes 6148
  104.3 6.1 %copy-start.4 = (bf16[2,2,256]{2,0,1:T(2,128)(2,1)}, bf16[2,2,256]{2,0,1:T(2,128)(2,1)S(1)}, u32[]{:S(2)}) copy-start(bf16[2,2,256]{2,0,1:T(2,128)(2,1)S(1)} %get-tuple-element.5) | copy-start | bytes 6148
  104.5 2.9 %copy-start.2 = (bf16[1,2048,512]{2,1,0:T(8,128)(2,1)S(1)}, bf16[1,2048,512]{2,1,0:T(8,128)(2,1)}, u32[]{:S(2)}) copy-start(bf16[1,2048,512]{2,1,0:T(8,128)(2,1)} %param.17) | copy-start | bytes 6291460
Sparse Core Ops, SparseCore 0:
  21.1 75.7 all-reduce.5
  155.0 17.0 all-reduce.3
where the time goes:
time: 181 us
  waiting for transfers between devices  90.7 us (50%)
  blocking collectives  38.4 us (21%)
  matrix products  23.7 us (13%)
  between operations  15.9 us (9%)
  other arithmetic  7.93 us (4%)
  local copies, waits for them, and re-layouts  4.07 us (2%)
    unnamed x3, waiting for transfers between devices  73.4 us
    all_gather x1, blocking collectives, per_device(): gathered = lax.all_gather(head_pair, 'gx', axis=0, tiled=True)  30.9 us
    psum x1, waiting for transfers between devices, per_device(): lax.psum(partial_out.astype(jnp.bfloat16), 'yz').astype(jnp.float32)  17.3 us
    dot_general x1, matrix products, per_device(): jnp.dot(gathered, output_weight, preferred_element_type=jnp.float32)  9.41 us
    dot_general x1, matrix products, per_device(): jnp.dot(scaled, query_weight, preferred_element_type=jnp.float32)  8.84 us
    all_to_all x1, blocking collectives, per_device(): lax.all_to_all(packed.reshape(halves, STEPS, cols), 'yz', split_axis=0, c...  3.75 us
    all_to_all x1, blocking collectives, per_device(): lax.all_to_all(attended, 'yz', split_axis=1, concat_axis=0, tiled=True)  3.75 us
  transfers between devices with their start and end apart: 2, of which 2 were waited for; matrix products, arithmetic and copies ran while one was open for 1% of the time, Pallas kernels for 0%

commit v1 on v0

v1 whole, which is shorter than its diff:
```python
import functools

import jax
import jax.numpy as jnp
from jax import lax
from jax.experimental import pallas as pl
from jax.experimental.pallas import tpu as pltpu
from jax.sharding import PartitionSpec as P

MODEL_WIDTH = 16384
HEAD_SIZE = 128
STEPS = 2
GROUP = 16
CHUNK = 512
OUT_PARTS = 4
MESH = pl.DeviceIdType.MESH


def remote(src, dst, send_sem, recv_sem, device):
    return pltpu.make_async_remote_copy(
        src_ref=src,
        dst_ref=dst,
        send_sem=send_sem,
        recv_sem=recv_sem,
        device_id=device,
        device_id_type=MESH,
    )


def kernel(
    n,
    rows_ref,
    x_ref,
    gain_ref,
    freq_ref,
    lengths_ref,
    positions_ref,
    qw_hbm,
    kw_hbm,
    vw_hbm,
    ow_hbm,
    kc_hbm,
    vc_hbm,
    out_ref,
    newk_ref,
    newv_ref,
    weights,
    kc,
    vc,
    ow,
    scaled,
    part,
    recv,
    sq_part,
    sq_recv,
    turned,
    q_send,
    q_all,
    att,
    gathered,
    wide,
    lhs,
    p_send,
    p_recv,
    w_sem,
    c_sem,
    o_sem,
    rs_send,
    rs_recv,
    sq_ssem,
    sq_rsem,
    q_ssem,
    q_rsem,
    g_ssem,
    g_rsem,
    p_ssem,
    p_rsem,
):
    me = lax.axis_index("gx")
    core = lax.axis_index("yz")
    other = 1 - core
    flat = me * 2 + core
    chunks = weights.shape[0]
    q_chunks = chunks - 1
    key_cols = kw_hbm.shape[1]
    out_cols = ow.shape[2]
    every = 2 * n

    for c in range(q_chunks):
        pltpu.make_async_copy(
            qw_hbm.at[:, c * CHUNK : (c + 1) * CHUNK], weights.at[c], w_sem.at[c]
        ).start()
    last = weights.at[q_chunks]
    pltpu.make_async_copy(kw_hbm, last.at[:, :key_cols], w_sem.at[q_chunks]).start()
    pltpu.make_async_copy(vw_hbm, last.at[:, key_cols:], w_sem.at[q_chunks]).start()
    pltpu.make_async_copy(kc_hbm, kc, c_sem.at[0]).start()
    pltpu.make_async_copy(vc_hbm, vc, c_sem.at[1]).start()
    for c in range(OUT_PARTS):
        pltpu.make_async_copy(
            ow_hbm.at[:, c * out_cols : (c + 1) * out_cols], ow.at[c], o_sem.at[c]
        ).start()

    barrier = pltpu.get_barrier_semaphore()

    def greet(t, carry):
        target = lax.rem(flat + t, every)
        pl.semaphore_signal(
            barrier,
            inc=1,
            device_id={"gx": target // 2, "yz": lax.rem(target, 2)},
            device_id_type=MESH,
        )
        return carry

    lax.fori_loop(1, every, greet, 0)

    xf = rows_ref[...].astype(jnp.float32)
    squares = jnp.sum(xf * xf, axis=1, keepdims=True)
    squares = jnp.broadcast_to(squares, (squares.shape[0], HEAD_SIZE))
    scaled[...] = (xf * gain_ref[...]).astype(jnp.bfloat16)
    for g in range(n):
        sq_part[g] = squares[4 * g : 4 * g + 4]
    turned[...] = jnp.zeros_like(turned)

    pl.semaphore_wait(barrier, every - 1)

    def sq_copy(d):
        target = lax.rem(me + d, n)
        return remote(
            sq_part.at[target], sq_recv.at[me], sq_ssem.at[d], sq_rsem.at[d], {"gx": target}
        )

    def rs_copy(d, c):
        target = lax.rem(me + d, n)
        return remote(
            part.at[target, c], recv.at[me, c], rs_send.at[d], rs_recv.at[d], {"gx": target}
        )

    def send_sq(d, carry):
        sq_copy(d).start()
        return carry

    lax.fori_loop(1, n, send_sq, 0)

    def project(c, carry):
        pltpu.make_async_copy(weights.at[c], weights.at[c], w_sem.at[c]).wait()
        result = jnp.dot(scaled[...], weights[c], preferred_element_type=jnp.float32)
        for g in range(n):
            part[g, c] = result[4 * g : 4 * g + 4]

        def send(d, inner):
            rs_copy(d, c).start()
            return inner

        lax.fori_loop(1, n, send, 0)
        return carry

    lax.fori_loop(0, chunks, project, 0)

    row_id = lax.broadcasted_iota(jnp.int32, (4, HEAD_SIZE), 0)
    first = positions_ref[2 * me]
    second = positions_ref[2 * me + 1]
    offsets = jnp.where(row_id < 2, first, second) + lax.rem(row_id, 2)
    angles = offsets.astype(jnp.float32) * freq_ref[...]
    lane = lax.broadcasted_iota(jnp.int32, (4, HEAD_SIZE), 1)
    cosine = jnp.cos(angles)
    sine = jnp.sin(angles)
    sine = jnp.where(lane < HEAD_SIZE // 2, -sine, sine)

    sq_recv[me] = sq_part[me]
    recv[me] = part[me]

    def arrive(d, carry):
        source = lax.rem(me + n - d, n)
        sq_copy(d).wait()
        whole = remote(
            part.at[lax.rem(me + d, n)],
            recv.at[source],
            rs_send.at[d],
            rs_recv.at[d],
            {"gx": lax.rem(me + d, n)},
        )
        whole.wait()
        return carry

    lax.fori_loop(1, n, arrive, 0)

    inverse = lax.rsqrt(jnp.sum(sq_recv[...], axis=0) / MODEL_WIDTH + 1e-05)
    heads_in_chunk = CHUNK // HEAD_SIZE
    for c in range(chunks):
        sums = jnp.sum(recv[:, c], axis=0)
        for k in range(heads_in_chunk):
            value = sums[:, k * HEAD_SIZE : (k + 1) * HEAD_SIZE] * inverse
            is_value = c == q_chunks and k >= heads_in_chunk // 2
            if not is_value:
                value = value * cosine + pltpu.roll(value, HEAD_SIZE // 2, 1) * sine
            if c < q_chunks:
                head = c * heads_in_chunk + k
                group, at = head // GROUP, 2 * (head % GROUP)
            else:
                group, at = k % 2, 48 if is_value else 32
            for r in range(2):
                turned[r, group, at : at + 2, :] = value[2 * r : 2 * r + 2]

    q_send[...] = turned[other].astype(jnp.bfloat16)
    swap = remote(q_send, q_all.at[core], q_ssem, q_rsem, {"yz": other})
    swap.start()
    q_all[core] = turned[core].astype(jnp.bfloat16)

    pltpu.make_async_copy(kc_hbm, kc, c_sem.at[0]).wait()
    pltpu.make_async_copy(vc_hbm, vc, c_sem.at[1]).wait()

    length = lengths_ref[0]
    scale = HEAD_SIZE ** (-0.5)
    queries = STEPS * GROUP
    slots = kc.shape[0]
    valid = lax.broadcasted_iota(jnp.int32, (queries, slots), 1) < length
    seen = lax.broadcasted_iota(jnp.int32, (queries, 16), 1) <= lax.rem(
        lax.broadcasted_iota(jnp.int32, (queries, 16), 0), 2
    )

    def attend(half):
        for i in range(2):
            block = q_all[half, i]
            q, kn, vn = block[:queries], block[32:48], block[48:64]
            at = pl.ds(pl.multiple_of((half * 2 + i) * HEAD_SIZE, HEAD_SIZE), HEAD_SIZE)
            cached = scale * lax.dot_general(
                q, kc[:, at], (((1,), (1,)), ((), ())), preferred_element_type=jnp.float32
            )
            recent = scale * lax.dot_general(
                q, kn, (((1,), (1,)), ((), ())), preferred_element_type=jnp.float32
            )
            cached = jnp.where(valid, cached, -jnp.inf)
            recent = jnp.where(seen, recent, -jnp.inf)
            highest = jnp.maximum(
                jnp.max(cached, axis=1, keepdims=True), jnp.max(recent, axis=1, keepdims=True)
            )
            cached = jnp.exp(cached - highest)
            recent = jnp.exp(recent - highest)
            total = jnp.sum(cached, axis=1, keepdims=True) + jnp.sum(
                recent, axis=1, keepdims=True
            )
            weighted = jnp.dot(
                cached.astype(jnp.bfloat16), vc[:, at], preferred_element_type=jnp.float32
            ) + jnp.dot(recent.astype(jnp.bfloat16), vn, preferred_element_type=jnp.float32)
            att[half, i * queries : (i + 1) * queries, :] = (weighted / total).astype(
                jnp.bfloat16
            )

    def spread_copy(t):
        target = lax.rem(flat + t, every)
        half = lax.rem(target, 2)
        return remote(
            att.at[half],
            gathered.at[flat],
            g_ssem.at[t],
            g_rsem.at[t],
            {"gx": target // 2, "yz": half},
        )

    attend(core)
    gathered[flat] = att[core]

    def spread_own(k, carry):
        spread_copy(2 * k).start()
        return carry

    lax.fori_loop(1, n, spread_own, 0)
    swap.wait()
    attend(other)

    def spread_other(k, carry):
        spread_copy(2 * k + 1).start()
        return carry

    lax.fori_loop(0, n, spread_other, 0)

    for half in range(2):
        for i in range(2):
            at = (half * 2 + i) * HEAD_SIZE
            block = q_all[half, i].astype(jnp.float32)
            newk_ref[:, at : at + HEAD_SIZE] = block[32:34].astype(jnp.bfloat16)
            newv_ref[:, at : at + HEAD_SIZE] = block[48:50].astype(jnp.bfloat16)

    def landed(t, carry):
        source = lax.rem(flat + every - t, every)
        target = lax.rem(flat + t, every)
        half = lax.rem(target, 2)
        remote(
            att.at[half],
            gathered.at[source],
            g_ssem.at[t],
            g_rsem.at[t],
            {"gx": target // 2, "yz": half},
        ).wait()
        return carry

    lax.fori_loop(1, every, landed, 0)

    block_rows = gathered.shape[1]
    for f in range(every):
        wide[f * block_rows : (f + 1) * block_rows, :] = gathered[f].astype(jnp.float32)
    for head in range(block_rows // STEPS):
        for s in range(STEPS):
            taken = wide[pl.ds(head * STEPS + s, every, stride=block_rows), :]
            lhs[s * every : (s + 1) * every, head * HEAD_SIZE : (head + 1) * HEAD_SIZE] = (
                taken.astype(jnp.bfloat16)
            )

    def final_copy(c):
        return remote(p_send.at[c], p_recv.at[c], p_ssem.at[c], p_rsem.at[c], {"yz": other})

    for c in range(OUT_PARTS):
        pltpu.make_async_copy(
            ow_hbm.at[:, c * out_cols : (c + 1) * out_cols], ow.at[c], o_sem.at[c]
        ).wait()
        p_send[c] = jnp.dot(lhs[...], ow[c], preferred_element_type=jnp.float32).astype(
            jnp.bfloat16
        )
        final_copy(c).start()
    for c in range(OUT_PARTS):
        final_copy(c).wait()
        both = p_send[c].astype(jnp.float32) + p_recv[c].astype(jnp.float32)
        at = slice(c * out_cols, (c + 1) * out_cols)
        for s in range(STEPS):
            mixed = x_ref[s, :, at].astype(jnp.float32) + both[s * every : (s + 1) * every]
            out_ref[s, :, at] = mixed.astype(jnp.bfloat16)


def per_device(
    hidden,
    norm_gain,
    query_weight,
    key_matrix,
    value_matrix,
    output_weight,
    key_cache_rows,
    value_cache_rows,
    lengths,
    positions,
):
    rows, width = hidden.shape[1], hidden.shape[2]
    n = lax.axis_size("gx")
    chunks = query_weight.shape[1] // CHUNK + 1
    slots, cache_cols = key_cache_rows.shape[1:]
    heads = query_weight.shape[1] // HEAD_SIZE
    half = HEAD_SIZE // 2
    freq = 500000.0 ** (-2.0 * jnp.arange(half, dtype=jnp.float32) / HEAD_SIZE)
    freq = jnp.concatenate([freq, freq])[None, :]
    ordered = hidden.transpose(1, 0, 2).reshape(rows * STEPS, width)
    out_cols = width // OUT_PARTS
    vmem = pl.BlockSpec(memory_space=pltpu.VMEM)
    smem = pl.BlockSpec(memory_space=pltpu.SMEM)
    hbm = pl.BlockSpec(memory_space=pl.ANY)
    bf16, f32 = jnp.bfloat16, jnp.float32
    dma = pltpu.SemaphoreType.DMA
    out, new_k, new_v = pl.pallas_call(
        functools.partial(kernel, n),
        out_shape=(
            jax.ShapeDtypeStruct((STEPS, rows, width), bf16),
            jax.ShapeDtypeStruct((STEPS, cache_cols), bf16),
            jax.ShapeDtypeStruct((STEPS, cache_cols), bf16),
        ),
        in_specs=[vmem, vmem, vmem, vmem, smem, smem] + [hbm] * 6,
        out_specs=(vmem, vmem, vmem),
        scratch_shapes=[
            pltpu.VMEM((chunks, width, CHUNK), bf16),
            pltpu.VMEM((slots, cache_cols), bf16),
            pltpu.VMEM((slots, cache_cols), bf16),
            pltpu.VMEM((OUT_PARTS, output_weight.shape[0], out_cols), bf16),
            pltpu.VMEM((rows * STEPS, width), bf16),
            pltpu.VMEM((n, chunks, 4, CHUNK), f32),
            pltpu.VMEM((n, chunks, 4, CHUNK), f32),
            pltpu.VMEM((n, 4, HEAD_SIZE), f32),
            pltpu.VMEM((n, 4, HEAD_SIZE), f32),
            pltpu.VMEM((2, 2, 64, HEAD_SIZE), f32),
            pltpu.VMEM((2, 64, HEAD_SIZE), bf16),
            pltpu.VMEM((2, 2, 64, HEAD_SIZE), bf16),
            pltpu.VMEM((2, heads * STEPS, HEAD_SIZE), bf16),
            pltpu.VMEM((2 * n, heads * STEPS, HEAD_SIZE), bf16),
            pltpu.VMEM((2 * n * heads * STEPS, HEAD_SIZE), f32),
            pltpu.VMEM((rows * STEPS, heads * HEAD_SIZE), bf16),
            pltpu.VMEM((OUT_PARTS, rows * STEPS, out_cols), bf16),
            pltpu.VMEM((OUT_PARTS, rows * STEPS, out_cols), bf16),
            dma((chunks,)),
            dma((2,)),
            dma((OUT_PARTS,)),
            dma((n,)),
            dma((n,)),
            dma((n,)),
            dma((n,)),
            dma,
            dma,
            dma((2 * n,)),
            dma((2 * n,)),
            dma((OUT_PARTS,)),
            dma((OUT_PARTS,)),
        ],
        compiler_params=pltpu.CompilerParams(
            collective_id=0, has_side_effects=True, vmem_limit_bytes=56 * 2**20
        ),
    )(
        ordered,
        hidden,
        norm_gain[None, :],
        freq,
        lengths,
        positions,
        query_weight,
        key_matrix,
        value_matrix,
        output_weight,
        key_cache_rows.reshape(slots, cache_cols),
        value_cache_rows.reshape(slots, cache_cols),
    )
    return (out, new_k[:, None, :], new_v[:, None, :])


def solution(mesh):
    in_specs = (
        P(None, "rep", "gx"),
        P("gx"),
        P("gx", "yz"),
        P("gx", "yz"),
        P("gx", "yz"),
        P("yz", "gx"),
        P(("rep", "gx", "yz"), None, None),
        P(("rep", "gx", "yz"), None, None),
        P(("rep", "gx", "yz")),
        P("rep"),
    )
    out_specs = (
        P(None, "rep", "gx"),
        P(None, ("rep", "gx", "yz"), None),
        P(None, ("rep", "gx", "yz"), None),
    )
    return jax.shard_map(
        per_device, mesh=mesh, in_specs=in_specs, out_specs=out_specs, check_vma=False
    )
```

time: 181 us -> 45 us (0.25)
  waiting for transfers between devices: 90.7 us -> 0 us
  blocking collectives: 38.4 us -> 0 us
  Pallas kernels: 0 us -> 37.1 us
  matrix products: 23.7 us -> 0 us
  between operations: 15.9 us -> 1.29 us
  other arithmetic: 7.93 us -> 0.6 us
    unnamed x3 -> x0, waiting for transfers between devices: 73.4 us -> none
    pallas_call x0 -> x1, Pallas kernels: none -> 37.1 us  [per_device(): pl.pallas_call(functools.partial(kernel, n), out_shape=(jax.ShapeDtypeStr...]
    all_gather x1 -> x0, blocking collectives: 30.9 us -> none  [per_device(): gathered = lax.all_gather(head_pair, 'gx', axis=0, tiled=True)]
    dot_general x20 -> x0, matrix products: 23.7 us -> none  [the longest x1 9.41 us: per_device(): jnp.dot(gathered, output_weight, preferred_element_type=jnp.float32)]
    psum x1 -> x0, waiting for transfers between devices: 17.3 us -> none  [per_device(): lax.psum(partial_out.astype(jnp.bfloat16), 'yz').astype(jnp.float32)]
    all_to_all x2 -> x0, blocking collectives: 7.5 us -> none  [the longest x1 3.75 us: per_device(): lax.all_to_all(packed.reshape(halves, STEPS, cols), 'yz', split_axis=0, c...]
    unnamed x20 -> x3, local copies, waits for them, and re-layouts: 0.74 us -> 4.07 us
    convert_element_type x4 -> x0, other arithmetic: 2.73 us -> none  [the longest x1 1 us: per_device(): hidden.transpose(1, 0, 2).reshape(batch_rows * STEPS, width)]
  transfers between devices with their start and end apart: 2 -> 0, of which waited for: 2 -> 0; matrix products, arithmetic and copies ran while one was open for 1% -> 0% of each run, Pallas kernels for 0% -> 0%
where the time goes in v1:
time: 45 us; the launch traced here: 44.8 us
  Pallas kernels  37.1 us (82%)
  local copies, waits for them, and re-layouts  5.81 us (13%)
  between operations  1.29 us (3%)
  other arithmetic  0.6 us (1%)
    pallas_call x1, Pallas kernels, per_device(): pl.pallas_call(functools.partial(kernel, n), out_shape=(jax.ShapeDtypeStr...  37.1 us
    unnamed x3, local copies, waits for them, and re-layouts  4.07 us
    transpose x1, local copies, waits for them, and re-layouts, per_device(): ordered = hidden.transpose(1, 0, 2).reshape(rows * STEPS, width)  1.04 us

profile of v1, /device:TPU:0, one launch (start us, length us, event | category | flops | bytes accessed | tf_op | source)
XLA Modules:
  0.0 44.8 jit_solution(8572903832008550582)
XLA Ops:
  1.3 0.6 %maximum_bitcast_fusion.freq_ref = f32[1,128]{1,0:T(1,128)} fusion(f32[64]{0:T(128)S(1)} %multiply_power_fusion), kind=kLoop, calls=%fused_computation | loop fusion | flops 128 | bytes 768 | tf_op jit(solution)/shard_map/broadcast_in_dim | solution.py:349
  1.9 1.0 %copy.13 = bf16[16,2,2048]{2,1,0:T(2,128)(2,1)S(1)} copy(bf16[16,2,2048]{2,0,1:T(8,128)(2,1)} %bitcast.10) | data formatting | bytes 262144 | tf_op jit(solution)/shard_map/transpose | solution.py:350
  2.9 0.7 %reshape.15.rows_ref = bf16[32,2048]{1,0:T(8,128)(2,1)} reshape(bf16[16,2,2048]{2,1,0:T(2,128)(2,1)S(1)} %copy.13) | data formatting | bytes 262144 | tf_op jit(solution)/shard_map/reshape | solution.py:350
  3.6 37.1 %shard_map.121 = (bf16[2,16,2048]{2,1,0:T(8,128)(2,1)}, bf16[2,512]{1,0:T(2,128)(2,1)}, bf16[2,512]{1,0:T(2,128)(2,1)}) custom-call(bf16[32,2048]{1,0:T(8,128)(2,1)} %reshape.15.rows_ref, bf16[2,16,2048]{2,1,0:T(8,128)(2,1)} %x_ref.1, f32[1,2048]{1,0:T(1,128)} %bitcast.11, f32[1,128]{1,0:T(1,128)} %maximum_bitcast_fusion.freq_ref, s32[1]{0:T(128)S(6)} %copy.17.lengths_ref, ...), custom_call_target="tpu_custom_call" | custom-call | tf_op jit(solution)/shard_map/pallas_call | solution.py:357
  40.7 1.6 %copy.18 = bf16[2,16,2048]{2,1,0:T(8,128)(2,1)} copy(bf16[2,16,2048]{2,1,0:T(8,128)(2,1)} %get-tuple-element.12) | data formatting | bytes 262144
  42.3 1.3 %copy.19 = bf16[2,1,512]{2,0,1:T(2,128)(2,1)} copy(bf16[2,1,512]{2,0,1:T(2,128)(2,1)} %bitcast.13) | data formatting | bytes 4096
  43.6 1.2 %copy.20 = bf16[2,1,512]{2,0,1:T(2,128)(2,1)} copy(bf16[2,1,512]{2,0,1:T(2,128)(2,1)} %bitcast.12) | data formatting | bytes 4096
  (1 shorter events, 0.0 us)

commit v2 on v1

--- a/solution.py
+++ b/solution.py
@@ -1,4 +1,5 @@
 import functools
+import math
 
 import jax
 import jax.numpy as jnp
@@ -13,6 +14,7 @@
 GROUP = 16
 CHUNK = 512
 OUT_PARTS = 4
+LAG = 2
 MESH = pl.DeviceIdType.MESH
 
 
@@ -29,10 +31,8 @@
 
 def kernel(
     n,
-    rows_ref,
     x_ref,
     gain_ref,
-    freq_ref,
     lengths_ref,
     positions_ref,
     qw_hbm,
@@ -50,6 +50,8 @@
     ow,
     scaled,
     part,
+    mate_part,
+    mid,
     recv,
     sq_part,
     sq_recv,
@@ -65,6 +67,8 @@
     w_sem,
     c_sem,
     o_sem,
+    mate_send,
+    mate_recv,
     rs_send,
     rs_recv,
     sq_ssem,
@@ -85,6 +89,9 @@
     key_cols = kw_hbm.shape[1]
     out_cols = ow.shape[2]
     every = 2 * n
+    pairs = n // 2
+    high, low = me // 2, lax.rem(me, 2)
+    mate = me + 1 - 2 * low
 
     for c in range(q_chunks):
         pltpu.make_async_copy(
@@ -114,12 +121,13 @@
 
     lax.fori_loop(1, every, greet, 0)
 
-    xf = rows_ref[...].astype(jnp.float32)
-    squares = jnp.sum(xf * xf, axis=1, keepdims=True)
-    squares = jnp.broadcast_to(squares, (squares.shape[0], HEAD_SIZE))
-    scaled[...] = (xf * gain_ref[...]).astype(jnp.bfloat16)
-    for g in range(n):
-        sq_part[g] = squares[4 * g : 4 * g + 4]
+    for step in range(STEPS):
+        xf = x_ref[step].astype(jnp.float32)
+        squares = jnp.sum(xf * xf, axis=1, keepdims=True)
+        squares = jnp.broadcast_to(squares, (every, HEAD_SIZE))
+        scaled[step * every : (step + 1) * every] = (xf * gain_ref[...]).astype(jnp.bfloat16)
+        for g in range(n):
+            sq_part[g, 2 * step : 2 * step + 2] = squares[2 * g : 2 * g + 2]
     turned[...] = jnp.zeros_like(turned)
 
     pl.semaphore_wait(barrier, every - 1)
@@ -130,10 +138,19 @@
             sq_part.at[target], sq_recv.at[me], sq_ssem.at[d], sq_rsem.at[d], {"gx": target}
         )
 
+    def mate_copy(c):
+        return remote(
+            part.at[1 - low, c], mate_part.at[c], mate_send.at[c], mate_recv.at[c], {"gx": mate}
+        )
+
     def rs_copy(d, c):
-        target = lax.rem(me + d, n)
+        target = lax.rem(high + d, pairs)
         return remote(
-            part.at[target, c], recv.at[me, c], rs_send.at[d], rs_recv.at[d], {"gx": target}
+            mid.at[target, c],
+            recv.at[high, c],
+            rs_send.at[d],
+            rs_recv.at[d],
+            {"gx": target * 2 + low},
         )
 
     def send_sq(d, carry):
@@ -142,48 +159,66 @@
 
     lax.fori_loop(1, n, send_sq, 0)
 
-    def project(c, carry):
+    def project(c):
         pltpu.make_async_copy(weights.at[c], weights.at[c], w_sem.at[c]).wait()
         result = jnp.dot(scaled[...], weights[c], preferred_element_type=jnp.float32)
         for g in range(n):
-            part[g, c] = result[4 * g : 4 * g + 4]
+            for step in range(STEPS):
+                at = step * every + 2 * g
+                part[g % 2, c, g // 2, 2 * step : 2 * step + 2] = result[at : at + 2]
+        mate_copy(c).start()
+
+    def add_mate(c):
+        mate_copy(c).wait()
+        for p in range(pairs):
+            mid[p, c] = part[low, c, p] + mate_part[c, p]
 
         def send(d, inner):
             rs_copy(d, c).start()
             return inner
 
-        lax.fori_loop(1, n, send, 0)
-        return carry
-
-    lax.fori_loop(0, chunks, project, 0)
+        lax.fori_loop(1, pairs, send, 0)
+
+    def stage(c, carry):
+        pl.when(c < chunks)(lambda: project(c))
+        pl.when(c >= LAG)(lambda: add_mate(c - LAG))
+        return carry
+
+    lax.fori_loop(0, chunks + LAG, stage, 0)
 
     row_id = lax.broadcasted_iota(jnp.int32, (4, HEAD_SIZE), 0)
     first = positions_ref[2 * me]
     second = positions_ref[2 * me + 1]
-    offsets = jnp.where(row_id < 2, first, second) + lax.rem(row_id, 2)
-    angles = offsets.astype(jnp.float32) * freq_ref[...]
+    offsets = jnp.where(lax.rem(row_id, 2) == 0, first, second) + row_id // 2
     lane = lax.broadcasted_iota(jnp.int32, (4, HEAD_SIZE), 1)
+    index = lax.rem(lane, HEAD_SIZE // 2).astype(jnp.float32)
+    freq = jnp.exp(index * (-2.0 * math.log(500000.0) / HEAD_SIZE))
+    angles = offsets.astype(jnp.float32) * freq
     cosine = jnp.cos(angles)
     sine = jnp.sin(angles)
     sine = jnp.where(lane < HEAD_SIZE // 2, -sine, sine)
 
     sq_recv[me] = sq_part[me]
-    recv[me] = part[me]
+    recv[high] = mid[high]
+
+    def arrive_sq(d, carry):
+        sq_copy(d).wait()
+        return carry
+
+    lax.fori_loop(1, n, arrive_sq, 0)
 
     def arrive(d, carry):
-        source = lax.rem(me + n - d, n)
-        sq_copy(d).wait()
-        whole = remote(
-            part.at[lax.rem(me + d, n)],
-            recv.at[source],
+        target = lax.rem(high + d, pairs)
+        remote(
+            mid.at[target],
+            recv.at[lax.rem(high + pairs - d, pairs)],
             rs_send.at[d],
             rs_recv.at[d],
-            {"gx": lax.rem(me + d, n)},
-        )
-        whole.wait()
-        return carry
-
-    lax.fori_loop(1, n, arrive, 0)
+            {"gx": target * 2 + low},
+        ).wait()
+        return carry
+
+    lax.fori_loop(1, pairs, arrive, 0)
 
     inverse = lax.rsqrt(jnp.sum(sq_recv[...], axis=0) / MODEL_WIDTH + 1e-05)
     heads_in_chunk = CHUNK // HEAD_SIZE
@@ -200,7 +235,10 @@
             else:
                 group, at = k % 2, 48 if is_value else 32
             for r in range(2):
-                turned[r, group, at : at + 2, :] = value[2 * r : 2 * r + 2]
+                for step in range(STEPS):
+                    turned[r, group, at + step : at + step + 1, :] = value[
+                        2 * step + r : 2 * step + r + 1
+                    ]
 
     q_send[...] = turned[other].astype(jnp.bfloat16)
     swap = remote(q_send, q_all.at[core], q_ssem, q_rsem, {"yz": other})
@@ -325,6 +363,12 @@
         for s in range(STEPS):
             mixed = x_ref[s, :, at].astype(jnp.float32) + both[s * every : (s + 1) * every]
             out_ref[s, :, at] = mixed.astype(jnp.bfloat16)
+
+
+def hand_over(out_in, k_in, v_in, out, k, v):
+    out[...] = out_in[...]
+    k[...] = k_in[...]
+    v[...] = v_in[...]
 
 
 def per_device(
@@ -344,10 +388,6 @@
     chunks = query_weight.shape[1] // CHUNK + 1
     slots, cache_cols = key_cache_rows.shape[1:]
     heads = query_weight.shape[1] // HEAD_SIZE
-    half = HEAD_SIZE // 2
-    freq = 500000.0 ** (-2.0 * jnp.arange(half, dtype=jnp.float32) / HEAD_SIZE)
-    freq = jnp.concatenate([freq, freq])[None, :]
-    ordered = hidden.transpose(1, 0, 2).reshape(rows * STEPS, width)
     out_cols = width // OUT_PARTS
     vmem = pl.BlockSpec(memory_space=pltpu.VMEM)
     smem = pl.BlockSpec(memory_space=pltpu.SMEM)
@@ -361,7 +401,7 @@
             jax.ShapeDtypeStruct((STEPS, cache_cols), bf16),
             jax.ShapeDtypeStruct((STEPS, cache_cols), bf16),
         ),
-        in_specs=[vmem, vmem, vmem, vmem, smem, smem] + [hbm] * 6,
+        in_specs=[vmem, vmem, smem, smem] + [hbm] * 6,
         out_specs=(vmem, vmem, vmem),
         scratch_shapes=[
             pltpu.VMEM((chunks, width, CHUNK), bf16),
@@ -369,8 +409,10 @@
             pltpu.VMEM((slots, cache_cols), bf16),
             pltpu.VMEM((OUT_PARTS, output_weight.shape[0], out_cols), bf16),
             pltpu.VMEM((rows * STEPS, width), bf16),
-            pltpu.VMEM((n, chunks, 4, CHUNK), f32),
-            pltpu.VMEM((n, chunks, 4, CHUNK), f32),
+            pltpu.VMEM((2, chunks, n // 2, 4, CHUNK), f32),
+            pltpu.VMEM((chunks, n // 2, 4, CHUNK), f32),
+            pltpu.VMEM((n // 2, chunks, 4, CHUNK), f32),
+            pltpu.VMEM((n // 2, chunks, 4, CHUNK), f32),
             pltpu.VMEM((n, 4, HEAD_SIZE), f32),
             pltpu.VMEM((n, 4, HEAD_SIZE), f32),
             pltpu.VMEM((2, 2, 64, HEAD_SIZE), f32),
@@ -385,8 +427,10 @@
             dma((chunks,)),
             dma((2,)),
             dma((OUT_PARTS,)),
-            dma((n,)),
-            dma((n,)),
+            dma((chunks,)),
+            dma((chunks,)),
+            dma((n // 2,)),
+            dma((n // 2,)),
             dma((n,)),
             dma((n,)),
             dma,
@@ -400,10 +444,8 @@
             collective_id=0, has_side_effects=True, vmem_limit_bytes=56 * 2**20
         ),
     )(
-        ordered,
         hidden,
         norm_gain[None, :],
-        freq,
         lengths,
         positions,
         query_weight,
@@ -413,6 +455,16 @@
         key_cache_rows.reshape(slots, cache_cols),
         value_cache_rows.reshape(slots, cache_cols),
     )
+    out, new_k, new_v = pl.pallas_call(
+        hand_over,
+        out_shape=(
+            jax.ShapeDtypeStruct(out.shape, bf16),
+            jax.ShapeDtypeStruct(new_k.shape, bf16),
+            jax.ShapeDtypeStruct(new_v.shape, bf16),
+        ),
+        in_specs=[vmem] * 3,
+        out_specs=(vmem,) * 3,
+    )(out, new_k, new_v)
     return (out, new_k[:, None, :], new_v[:, None, :])
 
 

time: 45 us -> 38.7 us (0.86)
  local copies, waits for them, and re-layouts: 5.81 us -> 0 us
  other arithmetic: 0.6 us -> 0 us
    unnamed x3 -> x0, local copies, waits for them, and re-layouts: 4.07 us -> none
    pallas_call x0 -> x1, Pallas kernels: none -> 1.58 us  [per_device(): pl.pallas_call(hand_over, out_shape=(jax.ShapeDtypeStruct(out.shape, bf16...]
    pallas_call x1, Pallas kernels: 37.1 us -> 35.6 us  [per_device(): pl.pallas_call(functools.partial(kernel, n), out_shape=(jax.ShapeDtypeStr...]
    transpose x1 -> x0, local copies, waits for them, and re-layouts: 1.04 us -> none  [per_device(): ordered = hidden.transpose(1, 0, 2).reshape(rows * STEPS, width)]
    reshape x1 -> x0, local copies, waits for them, and re-layouts: 0.71 us -> none  [per_device(): ordered = hidden.transpose(1, 0, 2).reshape(rows * STEPS, width)]
    broadcast_in_dim x1 -> x0, other arithmetic: 0.59 us -> none  [per_device(): freq = jnp.concatenate([freq, freq])[None, :]]
where the time goes in v2:
time: 38.7 us; the launch traced here: 38.5 us
  Pallas kernels  37.2 us (96%)
  between operations  1.29 us (3%)
    pallas_call x1, Pallas kernels, per_device(): pl.pallas_call(functools.partial(kernel, n), out_shape=(jax.ShapeDtypeStr...  35.6 us
    pallas_call x1, Pallas kernels, per_device(): pl.pallas_call(hand_over, out_shape=(jax.ShapeDtypeStruct(out.shape, bf16...  1.58 us

profile of v2, /device:TPU:0, one launch (start us, length us, event | category | flops | bytes accessed | tf_op | source)
XLA Modules:
  0.0 38.5 jit_solution(14105502649560057915)
XLA Ops:
  1.3 35.6 %shard_map.121 = (bf16[2,16,2048]{2,1,0:T(8,128)(2,1)}, bf16[2,512]{1,0:T(2,128)(2,1)}, bf16[2,512]{1,0:T(2,128)(2,1)}) custom-call(bf16[2,16,2048]{2,1,0:T(8,128)(2,1)} %x_ref.1, f32[1,2048]{1,0:T(1,128)} %bitcast.7, s32[1]{0:T(128)S(6)} %copy.13.lengths_ref, s32[16]{0:T(128)} %positions_ref.1, bf16[2048,4096]{1,0:T(8,128)(2,1)} %qw_hbm.1, ...), custom_call_target="tpu_custom_call" | custom-call | tf_op jit(solution)/shard_map/pallas_call | solution.py:397
  36.9 1.6 %shard_map.122 = (bf16[2,16,2048]{2,1,0:T(8,128)(2,1)}, bf16[2,512]{1,0:T(2,128)(2,1)}, bf16[2,512]{1,0:T(2,128)(2,1)}) custom-call(bf16[2,16,2048]{2,1,0:T(8,128)(2,1)} %get-tuple-element.9.out_in, bf16[2,512]{1,0:T(2,128)(2,1)} %get-tuple-element.10.k_in, bf16[2,512]{1,0:T(2,128)(2,1)} %get-tuple-element.11.v_in), custom_call_target="tpu_custom_call" | custom-call | tf_op jit(solution)/shard_map/pallas_call | solution.py:458

commit v3 on v2

--- a/solution.py
+++ b/solution.py
@@ -15,6 +15,7 @@
 CHUNK = 512
 OUT_PARTS = 4
 LAG = 2
+AHEAD = 4
 MESH = pl.DeviceIdType.MESH
 
 
@@ -93,19 +94,34 @@
     high, low = me // 2, lax.rem(me, 2)
     mate = me + 1 - 2 * low
 
-    for c in range(q_chunks):
-        pltpu.make_async_copy(
-            qw_hbm.at[:, c * CHUNK : (c + 1) * CHUNK], weights.at[c], w_sem.at[c]
-        ).start()
-    last = weights.at[q_chunks]
-    pltpu.make_async_copy(kw_hbm, last.at[:, :key_cols], w_sem.at[q_chunks]).start()
-    pltpu.make_async_copy(vw_hbm, last.at[:, key_cols:], w_sem.at[q_chunks]).start()
-    pltpu.make_async_copy(kc_hbm, kc, c_sem.at[0]).start()
-    pltpu.make_async_copy(vc_hbm, vc, c_sem.at[1]).start()
-    for c in range(OUT_PARTS):
+    def fetch_query(c):
+        at = pl.ds(pl.multiple_of(c * CHUNK, CHUNK), CHUNK)
+        pltpu.make_async_copy(qw_hbm.at[:, at], weights.at[c], w_sem.at[c]).start()
+
+    def fetch_new():
+        last = weights.at[q_chunks]
+        pltpu.make_async_copy(kw_hbm, last.at[:, :key_cols], w_sem.at[q_chunks]).start()
+        pltpu.make_async_copy(vw_hbm, last.at[:, key_cols:], w_sem.at[q_chunks]).start()
+
+    def fetch_caches():
+        pltpu.make_async_copy(kc_hbm, kc, c_sem.at[0]).start()
+        pltpu.make_async_copy(vc_hbm, vc, c_sem.at[1]).start()
+
+    def fetch_output(c):
         pltpu.make_async_copy(
             ow_hbm.at[:, c * out_cols : (c + 1) * out_cols], ow.at[c], o_sem.at[c]
         ).start()
+
+    def fetch_later(c):
+        pl.when(c + AHEAD < q_chunks)(lambda: fetch_query(c + AHEAD))
+        pl.when(c + AHEAD == q_chunks)(fetch_new)
+        pl.when(c + AHEAD == q_chunks + 1)(fetch_caches)
+        for k in range(OUT_PARTS):
+            turn = min(q_chunks + 2 + k - AHEAD, chunks - 1)
+            pl.when(c == turn)(functools.partial(fetch_output, k))
+
+    for c in range(AHEAD):
+        fetch_query(c)
 
     barrier = pltpu.get_barrier_semaphore()
 
@@ -161,6 +177,7 @@
 
     def project(c):
         pltpu.make_async_copy(weights.at[c], weights.at[c], w_sem.at[c]).wait()
+        fetch_later(c)
         result = jnp.dot(scaled[...], weights[c], preferred_element_type=jnp.float32)
         for g in range(n):
             for step in range(STEPS):

time: 38.7 us -> 38.7 us (level)
  no operation moved by 1% of the time
where the time goes in v3:
time: 38.7 us; the launch traced here: 38.5 us
  Pallas kernels  37.2 us (96%)
  between operations  1.29 us (3%)
    pallas_call x1, Pallas kernels, per_device(): pl.pallas_call(functools.partial(kernel, n), out_shape=(jax.ShapeDtypeStr...  35.6 us
    pallas_call x1, Pallas kernels, per_device(): pl.pallas_call(hand_over, out_shape=(jax.ShapeDtypeStruct(out.shape, bf16...  1.58 us

profile of v3, /device:TPU:0, one launch (start us, length us, event | category | flops | bytes accessed | tf_op | source)
XLA Modules:
  0.0 38.5 jit_solution(5363596149839180070)
XLA Ops:
  1.3 35.6 %shard_map.121 = (bf16[2,16,2048]{2,1,0:T(8,128)(2,1)}, bf16[2,512]{1,0:T(2,128)(2,1)}, bf16[2,512]{1,0:T(2,128)(2,1)}) custom-call(bf16[2,16,2048]{2,1,0:T(8,128)(2,1)} %x_ref.1, f32[1,2048]{1,0:T(1,128)} %bitcast.7, s32[1]{0:T(128)S(6)} %copy.13.lengths_ref, s32[16]{0:T(128)} %positions_ref.1, bf16[2048,4096]{1,0:T(8,128)(2,1)} %qw_hbm.1, ...), custom_call_target="tpu_custom_call" | custom-call | tf_op jit(solution)/shard_map/pallas_call | solution.py:414
  36.9 1.6 %shard_map.122 = (bf16[2,16,2048]{2,1,0:T(8,128)(2,1)}, bf16[2,512]{1,0:T(2,128)(2,1)}, bf16[2,512]{1,0:T(2,128)(2,1)}) custom-call(bf16[2,16,2048]{2,1,0:T(8,128)(2,1)} %get-tuple-element.9.out_in, bf16[2,512]{1,0:T(2,128)(2,1)} %get-tuple-element.10.k_in, bf16[2,512]{1,0:T(2,128)(2,1)} %get-tuple-element.11.v_in), custom_call_target="tpu_custom_call" | custom-call | tf_op jit(solution)/shard_map/pallas_call | solution.py:475
